TPU v7x, 32 devices: a whole 2x2x4 slice. The times are simulated.
32 devices in a mesh: group: 2 (over y), frame: 4 (over z), head: 2 (over x), sub: 2 (over core).
Axes of the slice: x: 2, y: 2, z: 4, core: 2. Of those that a mesh axis runs over, the one named last changes fastest.
Arguments:
- queries: bfloat16 [6144, 2560], P(('group', 'frame', 'sub'), 'head'), parts along dimension 0, may hold values from -12 to 12
- keys: bfloat16 [6144, 2560], P(('group', 'frame', 'sub'), 'head'), parts along dimension 0, may hold values from -4 to 4
- values: bfloat16 [6144, 2560], P(('group', 'frame', 'sub'), 'head'), parts along dimension 0, may hold values from -6 to 6
- out_weight: bfloat16 [2560, 5120], P(('frame', 'sub'), 'head'), may hold values from -0.125 to 0.125
- time_table: bfloat16 [50, 5120], P(None, 'head'), may hold values from -4 to 4
- action_table: bfloat16 [256, 5120], P(None, 'head'), may hold values from -4 to 4
- levels: int32 [8], P('group'), parts along dimension 0, may hold values from 0 to 49
- actions: int32 [8, 4], P('group'), parts along dimension 0, may hold values from 0 to 255
- cycle_order: int32 [8], P('group'), parts along dimension 0, may hold values from 0 to 3, as said below
Outputs:
- velocity: bfloat16 [6144, 5120], P(('group', 'frame', 'sub'), 'head'), parts along dimension 0
There are 2 independent parts, one for each index of `group`. A program takes and returns all parts, laid end to end along the dimension named above; an argument that names none is the same for every part. Nothing has to cross between parts.
Inputs may be any that keep to these rules, and one draw needn't show every extreme that they name: cycle_order[s] = (s + R) mod 4 for one R of the draw; each position appears once.
All inputs are finite; a program needn't handle non-finite values.
Results may differ from a plain program's by a relative error of at most 0.0056.
Values may be sent and summed in bfloat16 or wider, within the bound.
A program may use at most 64 MiB of HBM per device.

v0:
```python
import jax
import jax.numpy as jnp
from jax import lax
from jax.sharding import PartitionSpec as P

HEAD_DIM = 128
LEVELS = 50
ACTIONS = 256
FWIN = 3


def from_behind(array, axis, by):
    count = lax.axis_size(axis)
    return lax.ppermute(array, axis, [(i, (i + by) % count) for i in range(count)])


def attend_heads(query_rows, key_rows, value_rows, key_valid):
    query_count = query_rows.shape[0]
    length = key_rows.shape[0]
    row_width = query_rows.shape[1]
    head_count = row_width // HEAD_DIM
    query_heads = jnp.moveaxis(query_rows.reshape(query_count, head_count, HEAD_DIM), 1, 0)
    key_heads = jnp.moveaxis(key_rows.reshape(length, head_count, HEAD_DIM), 1, 0)
    value_heads = jnp.moveaxis(value_rows.reshape(length, head_count, HEAD_DIM), 1, 0)
    factor = HEAD_DIM ** (-0.5)

    def one_head(operands):
        query_one, key_one, value_one = operands
        scores = jnp.dot(query_one, key_one.T, preferred_element_type=jnp.float32) * factor
        scores = jnp.where(key_valid[None, :], scores, -1e30)
        largest = jnp.max(scores, axis=1, keepdims=True)
        weights = jnp.exp(scores - largest)
        totals = jnp.sum(weights, axis=1, keepdims=True)
        mixed_rows = jnp.dot(
            weights.astype(jnp.bfloat16), value_one, preferred_element_type=jnp.float32
        )
        return (mixed_rows / totals).astype(jnp.bfloat16)

    result = lax.map(one_head, (query_heads, key_heads, value_heads))
    return jnp.moveaxis(result, 0, 1).reshape(query_count, row_width)


def shards(
    queries, keys, values, out_weight, time_table, action_table, levels, actions, cycle_order
):
    window = FWIN
    frame_slot = lax.axis_index("frame")
    own_position = cycle_order[frame_slot]
    level_onehot = (jnp.arange(LEVELS, dtype=jnp.int32) == levels[frame_slot]).astype(jnp.bfloat16)
    action_match = jnp.arange(ACTIONS, dtype=jnp.int32)[None, :] == actions[frame_slot][:, None]
    action_count = jnp.sum(action_match.astype(jnp.float32), axis=0).astype(jnp.bfloat16)
    gate_row = jnp.dot(level_onehot[None, :], time_table, preferred_element_type=jnp.float32)
    gate_row = gate_row + jnp.dot(
        action_count[None, :], action_table, preferred_element_type=jnp.float32
    )
    paired = jnp.stack([keys, values])
    block_rows = paired.shape[1] * lax.axis_size("sub")
    local_pair = lax.all_gather(paired, "sub", axis=1, tiled=True)
    blocks = [local_pair]
    for distance in range(1, window):
        blocks.append(from_behind(local_pair, "frame", distance))
    joined = jnp.concatenate(blocks, axis=1)
    block_valid = own_position >= jnp.arange(window, dtype=jnp.int32)
    key_valid = jnp.repeat(block_valid, block_rows)
    attended = attend_heads(queries, joined[0], joined[1], key_valid)
    outputs = lax.all_gather(attended, "head", axis=1, tiled=True)
    all_rows = lax.all_gather(out_weight, ("frame", "sub"), axis=0, tiled=True)
    projected = jnp.dot(outputs, all_rows, preferred_element_type=jnp.float32)
    return (gate_row * projected).astype(jnp.bfloat16)


def solution(mesh):
    in_specs = (
        P(("group", "frame", "sub"), "head"),
        P(("group", "frame", "sub"), "head"),
        P(("group", "frame", "sub"), "head"),
        P(("frame", "sub"), "head"),
        P(None, "head"),
        P(None, "head"),
        P("group"),
        P("group", None),
        P("group"),
    )
    out_specs = P(("group", "frame", "sub"), "head")
    return jax.shard_map(shards, mesh=mesh, in_specs=in_specs, out_specs=out_specs, check_vma=False)
```

profile of v0, /device:TPU:1, one launch (start us, length us, event | category | flops | bytes accessed | tf_op | source)
XLA Modules:
  0.0 508.4 jit_solution(7207016949690037372)
XLA Ops:
  6.5 1.7 copy.18
  8.2 1.6 copy.19
  9.8 1.5 pad_maximum_fusion
  11.4 15.7 %all-gather.4.cloned.1.call-done = bf16[2,768,1280]{1,2,0:T(8,128)(2,1)} async-done(((bf16[2,384,1280]{1,2,0:T(8,128)(2,1)}), bf16[2,768,1280]{1,2,0:T(8,128)(2,1)}) %all-gather.4.cloned.1.call-update) | async-done | bytes 3932176 | tf_op jit(solution)/shard_map/all_gather | solution.py:58
  27.1 1.6 collective-permute-start
  28.7 2.1 collective-permute-start.1
  30.8 1.6 copy.17
  32.4 0.6 dynamic_slice.22
  33.0 0.6 iota_compare_fusion.1
  33.6 2.4 constant_dynamic-update-slice_fusion.3
  36.0 79.8 %collective-permute-done = bf16[2,768,1280]{1,2,0:T(8,128)(2,1)} collective-permute-done((bf16[2,768,1280]{1,2,0:T(8,128)(2,1)}, bf16[2,768,1280]{1,2,0:T(8,128)(2,1)}, u32[]{:S(2)}, u32[]{:S(2)}) %collective-permute-start) | collective-permute-done | bytes 3932192 | tf_op jit(solution)/shard_map/ppermute | solution.py:14
  115.8 2.4 constant_dynamic-update-slice_fusion.2
  118.2 166.6 %collective-permute-done.1 = bf16[2,768,1280]{1,2,0:T(8,128)(2,1)} collective-permute-done((bf16[2,768,1280]{1,2,0:T(8,128)(2,1)}, bf16[2,768,1280]{1,2,0:T(8,128)(2,1)}, u32[]{:S(2)}, u32[]{:S(2)}) %collective-permute-start.1) | collective-permute-done | bytes 3932192 | tf_op jit(solution)/shard_map/ppermute | solution.py:14
  284.8 2.4 constant_dynamic-update-slice_fusion.1
  287.2 4.7 fusion.31
  291.8 45.1 %while.11 = (s32[]{:T(128)}, bf16[10,384,128]{1,2,0:T(8,128)(2,1)S(1)}, bf16[10,384,128]{1,2,0:T(8,128)(2,1)S(1)}, bf16[10,2304,128]{1,2,0:T(8,128)(2,1)}, bf16[...) while((s32[]{:T(128)}, bf16[10,384,128]{1,2,0:T(8,128)(2,1)S(1)}, ...), condition=%wide.region_4.5_spmd.clone, body=%wide.region_1.4_spmd.clone.sunk | while | flops 459275520 | bytes 12405588 | solution.py:39
  291.9 1.8 fusion.44
  293.8 0.6 fusion.45
  294.4 1.8 fusion.46
  296.2 0.1 copy.30
  296.4 1.8 fusion.44
  298.3 0.6 fusion.45
  298.9 1.8 fusion.46
  300.7 0.1 copy.30
  300.9 1.8 fusion.44
  302.8 0.6 fusion.45
  303.4 1.8 fusion.46
  305.2 0.1 copy.30
  305.5 1.8 fusion.44
  307.3 0.6 fusion.45
  307.9 1.8 fusion.46
  309.7 0.1 copy.30
  310.0 1.8 fusion.44
  311.8 0.6 fusion.45
  312.4 1.8 fusion.46
  314.2 0.1 copy.30
  314.5 1.8 fusion.44
  316.3 0.6 fusion.45
  317.0 1.8 fusion.46
  318.7 0.1 copy.30
  319.0 1.8 fusion.44
  320.8 0.6 fusion.45
  321.5 1.8 fusion.46
  323.2 0.1 copy.30
  323.5 1.8 fusion.44
  325.4 0.6 fusion.45
  326.0 1.8 fusion.46
  327.7 0.1 copy.30
  328.0 1.8 fusion.44
  329.9 0.6 fusion.45
  330.5 1.8 fusion.46
  332.3 0.1 copy.30
  332.5 1.8 fusion.44
  334.4 0.6 fusion.45
  335.0 1.8 fusion.46
  337.0 0.9 copy-done.1
  338.0 0.7 all-gather.8.cloned.1.call-update
  338.7 0.7 dynamic-slice_bitcast_fusion
  339.4 0.7 dynamic_slice.20
  340.1 1.8 convolution_reduce_fusion.1
  341.9 0.3 convolution_reduce_fusion
  342.2 26.6 %all-gather.6.cloned.1.call-done = bf16[384,2560]{0,1:T(8,128)(2,1)} async-done(((bf16[384,1280]{0,1:T(8,128)(2,1)}), bf16[384,2560]{0,1:T(8,128)(2,1)}) %all-gather.6.cloned.1.call-update) | async-done | bytes 1966096 | tf_op jit(solution)/shard_map/all_gather | solution.py:66
  368.8 123.1 %all-gather.8.cloned.1.call-done = bf16[2560,2560]{1,0:T(8,128)(2,1)} async-done(((bf16[320,2560]{1,0:T(8,128)(2,1)}), bf16[2560,2560]{1,0:T(8,128)(2,1)}) %all-gather.8.cloned.1.call-update) | async-done | bytes 13107216 | tf_op jit(solution)/shard_map/all_gather | solution.py:67
  492.0 9.9 %fusion.25 = bf16[384,2560]{1,0:T(8,128)(2,1)} fusion(bf16[384,2560]{0,1:T(8,128)(2,1)} %all-gather.6.cloned.1.call-done, bf16[2560,2560]{1,0:T(8,128)(2,1)} %all-gather.8.cloned.1.call-done, f32[2560]{0:T(1024)S(1)} %add.13), kind=kOutput, calls=%fused_computation.21 | convolution fusion | flops 5035130880 | bytes 17049600 | tf_op jit(solution)/shard_map/dot_general | solution.py:68
  (47 shorter events, 1.6 us)
Async XLA Ops:
  6.5 335.4 %copy-start = (bf16[256,2560]{1,0:T(8,128)(2,1)S(1)}, bf16[256,2560]{1,0:T(8,128)(2,1)}, u32[]{:S(2)}) copy-start(bf16[256,2560]{1,0:T(8,128)(2,1)} %param.16) | copy-start | bytes 3932164
  6.5 20.6 %all-gather.4.cloned.1.call-start = ((), (), s32[]{:S(2)}) async-start(), calls=%async_computation | async-start | bytes 5898240 | tf_op jit(solution)/shard_map/all_gather | solution.py:58
  9.8 22.6 %copy-start.2 = (s32[4]{0:T(128)S(1)}, s32[4]{0:T(128)}, u32[]{:S(2)}) copy-start(s32[4]{0:T(128)} %param.19) | copy-start | bytes 52
  11.3 357.5 %all-gather.6.cloned.1.call-start = ((), (), s32[]{:S(2)}) async-start(), calls=%async_computation.1 | async-start | bytes 2949120 | tf_op jit(solution)/shard_map/all_gather | solution.py:66
  27.1 88.7 %collective-permute-start = (bf16[2,768,1280]{1,2,0:T(8,128)(2,1)}, bf16[2,768,1280]{1,2,0:T(8,128)(2,1)}, u32[]{:S(2)}, u32[]{:S(2)}) collective-permute-start(bf16[2,768,1280]{1,2,0:T(8,128)(2,1)} %all-gather.4.cloned.1.call-done), channel_id=1, source_target_pairs={{0,4},{4,8},{8,12},{12,0},{1,5},{5,9},{9,13},{13,1},{2,6},{6,10},{... | collective-permute-start | bytes 11796488 | tf_op jit(solution)/shard_map/ppermute | solution.py:14
  28.7 256.1 %collective-permute-start.1 = (bf16[2,768,1280]{1,2,0:T(8,128)(2,1)}, bf16[2,768,1280]{1,2,0:T(8,128)(2,1)}, u32[]{:S(2)}, u32[]{:S(2)}) collective-permute-start(bf16[2,768,1280]{1,2,0:T(8,128)(2,1)} %all-gather.4.cloned.1.call-done), channel_id=1, source_target_pairs={{0,8},{4,12},{8,0},{12,4},{1,9},{5,13},{9,1},{13,5},{2,10},{6,14},... | collective-permute-start | bytes 11796488 | tf_op jit(solution)/shard_map/ppermute | solution.py:14
  291.8 47.6 %copy-start.3 = (s32[4]{0:T(128)S(1)}, s32[4]{0:T(128)}, u32[]{:S(2)}) copy-start(s32[4]{0:T(128)} %param.17) | copy-start | bytes 52
  336.9 0.9 copy-start.1
  337.9 154.0 %all-gather.8.cloned.1.call-start = ((), (), s32[]{:S(2)}) async-start(), calls=%async_computation.2 | async-start | bytes 14745600 | tf_op jit(solution)/shard_map/all_gather | solution.py:67
Sparse Core Ops, SparseCore 0:
  11.5 15.6 all-gather.3
  338.0 30.7 all-gather.5
  370.5 121.4 all-gather.7
where the time goes:
time: 510 us; the launch traced here: 508 us
  waiting for transfers between devices  413 us (81%)
  matrix products  48.1 us (9%)
  local copies, waits for them, and re-layouts  22 us (4%)
  between operations  13.2 us (3%)
  other arithmetic  8.46 us (2%)
    ppermute x2, waiting for transfers between devices, from_behind(): lax.ppermute(array, axis, [(i, (i + by) % count) for i in range(count)])  246 us
    all_gather x1, waiting for transfers between devices, shards(): all_rows = lax.all_gather(out_weight, ('frame', 'sub'), axis=0, tiled=True)  123 us
    all_gather x1, waiting for transfers between devices, shards(): outputs = lax.all_gather(attended, 'head', axis=1, tiled=True)  26.6 us
    dot_general x10, matrix products, one_head(): jnp.dot(query_one, key_one.T, preferred_element_type=jnp.float32) * factor  18.5 us
    dot_general x10, matrix products, one_head(): jnp.dot(weights.astype(jnp.bfloat16), value_one, preferred_element_type=j...  17.7 us
    all_gather x1, waiting for transfers between devices, shards(): local_pair = lax.all_gather(paired, 'sub', axis=1, tiled=True)  15.7 us
    unnamed x13, local copies, waits for them, and re-layouts  10.5 us
  transfers between devices with their start and end apart: 5, of which 5 were waited for; matrix products, arithmetic and copies ran while one was open for 2% of the time, Pallas kernels for 0%

commit v1 on v0

--- a/solution.py
+++ b/solution.py
@@ -1,12 +1,19 @@
+import functools
+
 import jax
 import jax.numpy as jnp
 from jax import lax
+from jax.experimental import pallas as pl
+from jax.experimental.pallas import tpu as pltpu
 from jax.sharding import PartitionSpec as P
 
 HEAD_DIM = 128
 LEVELS = 50
 ACTIONS = 256
 FWIN = 3
+PIECES = 5
+LOG2E = 1.4426950408889634
+MESH = pl.DeviceIdType.MESH
 
 
 def from_behind(array, axis, by):
@@ -40,19 +47,23 @@
     return jnp.moveaxis(result, 0, 1).reshape(query_count, row_width)
 
 
-def shards(
-    queries, keys, values, out_weight, time_table, action_table, levels, actions, cycle_order
-):
-    window = FWIN
+def gate_of_slot(time_table, action_table, levels, actions):
     frame_slot = lax.axis_index("frame")
-    own_position = cycle_order[frame_slot]
     level_onehot = (jnp.arange(LEVELS, dtype=jnp.int32) == levels[frame_slot]).astype(jnp.bfloat16)
     action_match = jnp.arange(ACTIONS, dtype=jnp.int32)[None, :] == actions[frame_slot][:, None]
     action_count = jnp.sum(action_match.astype(jnp.float32), axis=0).astype(jnp.bfloat16)
     gate_row = jnp.dot(level_onehot[None, :], time_table, preferred_element_type=jnp.float32)
-    gate_row = gate_row + jnp.dot(
+    return gate_row + jnp.dot(
         action_count[None, :], action_table, preferred_element_type=jnp.float32
     )
+
+
+def ring_shards(
+    queries, keys, values, out_weight, time_table, action_table, levels, actions, cycle_order
+):
+    window = FWIN
+    own_position = cycle_order[lax.axis_index("frame")]
+    gate_row = gate_of_slot(time_table, action_table, levels, actions)
     paired = jnp.stack([keys, values])
     block_rows = paired.shape[1] * lax.axis_size("sub")
     local_pair = lax.all_gather(paired, "sub", axis=1, tiled=True)
@@ -69,6 +80,394 @@
     return (gate_row * projected).astype(jnp.bfloat16)
 
 
+class Indices:
+    def __init__(self, sems):
+        self.sems, self.names, self.used = sems, {}, 0
+
+    def __call__(self, name, count=1):
+        if name not in self.names:
+            self.names[name] = (self.used, count)
+            self.used += count
+        return self.names[name][0]
+
+
+def line_kernel(
+    cycle, q, k, v, w, gate, out,
+    kb, vb, qb, stat, acc, attf, aout, wf, pacc, send_sems, recv_sems, local_sems,
+):
+    rows, cols = q.shape
+    wrows, wide = w.shape
+    half = wrows // 2
+    part = half // PIECES
+    heads = cols // HEAD_DIM
+    per = heads // PIECES
+    att_cols = per * HEAD_DIM
+    keys_n = 2 * rows
+    scale = HEAD_DIM ** (-0.5) * LOG2E
+
+    g, f, h, c = (lax.axis_index(name) for name in ("group", "frame", "head", "sub"))
+    side = f // 2
+    f_in, f_out = 1 + side, 3 * side
+    peer_in, peer_out = 2 - side, 3 - 3 * side
+    inner = f == f_in
+    mate = f_in + f_out - f
+    sub_dev = (g, f, h, 1 - c)
+    x_dev = (g, f, 1 - h, c)
+    y_dev = (1 - g, f, h, c)
+    mate_dev = (g, mate, h, c)
+    peer_dev = (g, peer_in, h, c)
+
+    barrier = pltpu.get_barrier_semaphore()
+    for dev in (sub_dev, x_dev, y_dev, mate_dev):
+        pl.semaphore_signal(barrier, inc=1, device_id=dev, device_id_type=MESH)
+
+    @pl.when(inner)
+    def _():
+        pl.semaphore_signal(barrier, inc=1, device_id=peer_dev, device_id_type=MESH)
+        pl.semaphore_wait(barrier, 5)
+
+    @pl.when(jnp.logical_not(inner))
+    def _():
+        pl.semaphore_wait(barrier, 4)
+
+    sends, recvs = Indices(send_sems), Indices(recv_sems)
+
+    def copy(src, dst, send, recv, dev):
+        return pltpu.make_async_remote_copy(
+            src_ref=src,
+            dst_ref=dst,
+            send_sem=send_sems.at[send],
+            recv_sem=recv_sems.at[recv],
+            device_id=dev,
+            device_id_type=MESH,
+        )
+
+    def arrived(dst, recv):
+        copy(dst, dst, 0, recv, sub_dev).wait_recv()
+
+    def own_rows(base, count, index):
+        return pl.ds(pl.multiple_of(base + index * count, 16), count)
+
+    def kv_half(buf, block, cc):
+        return buf.at[block, own_rows(0, rows, cc), :]
+
+    def w_shard(block, cc):
+        return wf.at[block, own_rows(0, wrows, cc), :]
+
+    def w_piece(block, cc, gg):
+        return wf.at[block, own_rows(cc * wrows, half, gg), :]
+
+    def w_part(block, cc, gg, i):
+        return wf.at[block, own_rows(cc * wrows + gg * half, part, i), :]
+
+    def att_part(ref, i):
+        return ref.at[:, pl.ds(pl.multiple_of(i * att_cols, HEAD_DIM), att_cols)]
+
+    kv_z = lambda n, which: recvs("kvz" + n + which)
+    kv_s = lambda n, which: recvs("kvs" + n + which)
+    wz = {b: recvs("wz" + b, PIECES) for b in ("mate", "pi", "po")}
+    wy = {b: recvs("wy" + b, PIECES) for b in ("mate", "pi", "po")}
+    ws = {b: recvs("ws" + b, 2) for b in ("mate", "pi", "po")}
+    ws_own, rq = recvs("wsown"), recvs("q")
+    ra, rx = recvs("ra", PIECES), recvs("rx", PIECES)
+    wblock = {"mate": mate, "pi": peer_in, "po": peer_out}
+
+    def w_to_sub(b, gg, which):
+        src = w_piece(wblock[b], c, gg)
+        one = copy(src, src, sends("wsub" + b + str(which)), ws[b] + which, sub_dev)
+        one.start()
+
+    def w_piece_to_y(b):
+        src = w_piece(wblock[b], c, g)
+        copy(src, src, sends("wyp" + b, PIECES), wy[b], y_dev).start()
+
+    def w_part_to_y(b, i):
+        src = w_part(wblock[b], c, g, i)
+        copy(src, src, sends("wyp" + b, PIECES) + i, wy[b] + i, y_dev).start()
+
+    def w_part_to_mate(b, i):
+        src = w_part(wblock[b], c, g, i)
+        copy(src, src, sends("wout" + b, PIECES) + i, wz[b] + i, mate_dev).start()
+
+    def valid_of(slot, block):
+        distance = (slot - block + 4) % 4
+        return cycle[block] == cycle[slot] - distance
+
+    def unit(si, block, head, finish=None):
+        slot = jnp.where(si == 0, f_in, f_out)
+        valid = valid_of(slot, block)
+        lanes = pl.ds(pl.multiple_of(head * HEAD_DIM, HEAD_DIM), HEAD_DIM)
+        si_head = si * heads + head
+        scores = lax.dot_general(
+            qb[si, :, lanes], kb[block, :, lanes], (((1,), (1,)), ((), ())),
+            preferred_element_type=jnp.float32,
+        )
+        old = stat[si_head]
+        old_max, old_total = old[:, :1], old[:, 64:65]
+        block_max = jnp.where(valid, jnp.max(scores, axis=1, keepdims=True), -1e30)
+        new_max = jnp.maximum(old_max, block_max)
+        weights = jnp.exp2((scores - jnp.where(valid, new_max, 1e30)) * scale)
+        fade = jnp.exp2((old_max - new_max) * scale)
+        total = old_total * fade + jnp.sum(weights, axis=1, keepdims=True)
+        mixed = acc[si_head] * fade + jnp.dot(
+            weights.astype(jnp.bfloat16), vb[block, :, lanes], preferred_element_type=jnp.float32
+        )
+        if finish is None:
+            acc[si_head] = mixed
+            lane = lax.broadcasted_iota(jnp.int32, (rows, HEAD_DIM), 1)
+            stat[si_head] = jnp.where(lane < 64, new_max, total)
+        else:
+            finish[:, lanes] = (mixed / total).astype(jnp.bfloat16)
+
+    def units(si, block):
+        @pl.loop(0, heads)
+        def _(head):
+            unit(si, block, head)
+
+    def each_part(body):
+        @pl.loop(0, PIECES)
+        def _(i):
+            body(i)
+
+    own_w = pltpu.make_async_copy(w, w_shard(f, c), local_sems.at[0])
+    own_w.start()
+    w_to_partner = copy(w, w_shard(f, c), sends("wown"), ws_own, sub_dev)
+
+    @pl.when(inner)
+    def _():
+        for n, ref, buf in (("k", k, kb), ("v", v, vb)):
+            copy(ref, kv_half(buf, f, c), sends("i_sub" + n), kv_s(n, "i"), sub_dev).start()
+            copy(ref, kv_half(buf, f, c), sends("i_peer" + n), kv_z(n, "pi"), peer_dev).start()
+        locals_ = [
+            pltpu.make_async_copy(k, kv_half(kb, f, c), local_sems.at[1]),
+            pltpu.make_async_copy(v, kv_half(vb, f, c), local_sems.at[2]),
+            pltpu.make_async_copy(q, qb.at[0], local_sems.at[3]),
+        ]
+        for one in locals_:
+            one.start()
+        w_to_partner.start()
+        copy(
+            w.at[own_rows(0, half, g), :], w_piece(f, c, g), sends("w_in_out"), wz["mate"], mate_dev
+        ).start()
+
+        @pl.loop(0, 2 * heads)
+        def _(i):
+            acc[i] = jnp.zeros((rows, HEAD_DIM), jnp.float32)
+            lane = lax.broadcasted_iota(jnp.int32, (rows, HEAD_DIM), 1)
+            stat[i] = jnp.where(lane < 64, -1e30, 0.0)
+
+        for one in locals_:
+            one.wait()
+        for n, buf in (("k", kb), ("v", vb)):
+            arrived(kv_half(buf, f, 1 - c), kv_s(n, "i"))
+        units(0, f_in)
+        for n, buf in (("k", kb), ("v", vb)):
+            src = kv_half(buf, f_out, c)
+            arrived(src, kv_z(n, "o"))
+            copy(src, src, sends("o_peer" + n), kv_z(n, "po"), peer_dev).start()
+            copy(src, src, sends("o_sub" + n), kv_s(n, "o"), sub_dev).start()
+        for n, buf in (("k", kb), ("v", vb)):
+            src = kv_half(buf, peer_in, c)
+            arrived(src, kv_z(n, "pi"))
+            copy(src, src, sends("pi_sub" + n), kv_s(n, "pi"), sub_dev).start()
+        for n, buf in (("k", kb), ("v", vb)):
+            arrived(kv_half(buf, f_out, 1 - c), kv_s(n, "o"))
+            arrived(kv_half(buf, peer_in, 1 - c), kv_s(n, "pi"))
+        units(0, jnp.where(side == 0, f_out, peer_in))
+        arrived(qb.at[1], rq)
+        units(1, f_out)
+        units(1, peer_in)
+        arrived(w_piece(mate, c, g), wz["mate"])
+        w_piece_to_y("mate")
+        w_to_sub("mate", g, 0)
+        for n, buf in (("k", kb), ("v", vb)):
+            src = kv_half(buf, peer_out, c)
+            arrived(src, kv_z(n, "po"))
+            copy(src, src, sends("po_sub" + n), kv_s(n, "po"), sub_dev).start()
+        own_w.wait()
+
+        def w_to_peer(i):
+            src = w_part(f, c, g, i)
+            copy(src, src, sends("w_own_peer", PIECES) + i, wz["pi"] + i, peer_dev).start()
+
+        def mate_w_to_peer(i):
+            src = w_part(mate, c, g, i)
+            copy(src, src, sends("w_mate_peer", PIECES) + i, wz["po"] + i, peer_dev).start()
+
+        each_part(w_to_peer)
+        each_part(mate_w_to_peer)
+        for n, buf in (("k", kb), ("v", vb)):
+            arrived(kv_half(buf, peer_out, 1 - c), kv_s(n, "po"))
+        last_block = jnp.where(side == 0, peer_out, f_in)
+
+        def last(i):
+            @pl.loop(0, per)
+            def _(j):
+                unit(1, last_block, i * per + j, aout)
+                unit(0, peer_out, i * per + j, attf.at[h])
+
+            src = att_part(aout, i)
+            copy(src, att_part(attf.at[h], i), sends("aout", PIECES) + i, ra + i, mate_dev).start()
+            src = att_part(attf.at[h], i)
+            copy(src, src, sends("ax", PIECES) + i, rx + i, x_dev).start()
+            arrived(w_part(peer_in, c, g, i), wz["pi"] + i)
+            w_part_to_mate("pi", i)
+            w_part_to_y("pi", i)
+
+        each_part(last)
+        arrived(w_piece(mate, c, 1 - g), wy["mate"])
+        w_to_sub("mate", 1 - g, 1)
+        w_to_sub("pi", g, 0)
+
+        def po(i):
+            arrived(w_part(peer_out, c, g, i), wz["po"] + i)
+            w_part_to_mate("po", i)
+            w_part_to_y("po", i)
+
+        each_part(po)
+
+    @pl.when(jnp.logical_not(inner))
+    def _():
+        first = [
+            copy(k, kv_half(kb, f, c), sends("out_k"), kv_z("k", "o"), mate_dev),
+            copy(v, kv_half(vb, f, c), sends("out_v"), kv_z("v", "o"), mate_dev),
+        ]
+        for one in first:
+            one.start()
+        w_to_partner.start()
+        own_w.wait()
+        arrived(w_piece(mate, c, g), wz["mate"])
+        w_piece_to_y("mate")
+        w_to_sub("mate", g, 0)
+        for one in first:
+            one.wait_send()
+        q_copy = copy(q, qb.at[1], sends("out_q"), rq, mate_dev)
+        q_copy.start()
+        q_copy.wait_send()
+        src = w_piece(f, c, g)
+        w_copy = copy(src, src, sends("out_w"), wz["mate"], mate_dev)
+        w_copy.start()
+        arrived(w_piece(mate, c, 1 - g), wy["mate"])
+        w_to_sub("mate", 1 - g, 1)
+        w_copy.wait_send()
+
+        def pi(i):
+            src = att_part(attf.at[h], i)
+            arrived(src, ra + i)
+            copy(src, src, sends("ax", PIECES) + i, rx + i, x_dev).start()
+            arrived(w_part(peer_in, c, g, i), wz["pi"] + i)
+            w_part_to_y("pi", i)
+
+        each_part(pi)
+        w_to_sub("pi", g, 0)
+
+        def po(i):
+            arrived(w_part(peer_out, c, g, i), wz["po"] + i)
+            w_part_to_y("po", i)
+
+        each_part(po)
+
+    w_to_sub("po", g, 0)
+    each_part(lambda i: arrived(w_part(peer_in, c, 1 - g, i), wy["pi"] + i))
+    w_to_sub("pi", 1 - g, 1)
+    each_part(lambda i: arrived(att_part(attf.at[1 - h], i), rx + i))
+    arrived(w_shard(f, 1 - c), ws_own)
+    for b in ("mate", "pi"):
+        arrived(w_piece(wblock[b], 1 - c, g), ws[b])
+        arrived(w_piece(wblock[b], 1 - c, 1 - g), ws[b] + 1)
+
+    depth = 2 * wrows
+    tile = 512
+
+    def product(block, lanes):
+        att_lanes = pl.ds(pl.multiple_of((block % 2) * depth, HEAD_DIM), depth)
+        return jnp.dot(
+            attf[block // 2, :, att_lanes], wf[block, :, lanes], preferred_element_type=jnp.float32
+        )
+
+    @pl.loop(0, wide // tile)
+    def _(n):
+        lanes = pl.ds(pl.multiple_of(n * tile, tile), tile)
+        pacc[:, lanes] = product(f, lanes) + product(mate, lanes) + product(peer_in, lanes)
+
+    each_part(lambda i: arrived(w_part(peer_out, c, 1 - g, i), wy["po"] + i))
+    w_to_sub("po", 1 - g, 1)
+    arrived(w_piece(peer_out, 1 - c, g), ws["po"])
+    arrived(w_piece(peer_out, 1 - c, 1 - g), ws["po"] + 1)
+
+    @pl.loop(0, wide // tile)
+    def _(n):
+        lanes = pl.ds(pl.multiple_of(n * tile, tile), tile)
+        total = pacc[:, lanes] + product(peer_out, lanes)
+        out[:, lanes] = (total * gate[:, lanes]).astype(jnp.bfloat16)
+
+    def sent(src, name, offset=0):
+        copy(src, src, sends(name) + offset, 0, sub_dev).wait_send()
+
+    sent(w, "wown")
+    for b in ("mate", "pi", "po"):
+        for which in range(2):
+            sent(w_piece(0, 0, 0), "wsub" + b + str(which))
+    sent(w_piece(0, 0, 0), "wypmate")
+
+    def common_sent(i):
+        sent(att_part(aout, 0), "ax", i)
+        for b in ("pi", "po"):
+            sent(w_part(0, 0, 0, 0), "wyp" + b, i)
+
+    each_part(common_sent)
+
+    @pl.when(inner)
+    def _():
+        for n in "kv":
+            for name in ("i_sub", "i_peer", "o_peer", "o_sub", "pi_sub", "po_sub"):
+                sent(k, name + n)
+        sent(w_piece(0, 0, 0), "w_in_out")
+
+        def inner_sent(i):
+            sent(att_part(aout, 0), "aout", i)
+            for name in ("w_own_peer", "w_mate_peer", "woutpi", "woutpo"):
+                sent(w_part(0, 0, 0, 0), name, i)
+
+        each_part(inner_sent)
+
+    assert sends.used <= send_sems.shape[0] and recvs.used <= recv_sems.shape[0]
+
+
+def line_shards(
+    queries, keys, values, out_weight, time_table, action_table, levels, actions, cycle_order
+):
+    gate_row = gate_of_slot(time_table, action_table, levels, actions)
+    rows, cols = queries.shape
+    wrows, wide = out_weight.shape
+    heads = cols // HEAD_DIM
+    bf16, f32 = jnp.bfloat16, jnp.float32
+    vmem = pl.BlockSpec(memory_space=pltpu.VMEM)
+    return pl.pallas_call(
+        line_kernel,
+        out_shape=jax.ShapeDtypeStruct((rows, wide), bf16),
+        in_specs=[pl.BlockSpec(memory_space=pltpu.SMEM)] + [vmem] * 5,
+        out_specs=vmem,
+        scratch_shapes=[
+            pltpu.VMEM((4, 2 * rows, cols), bf16),
+            pltpu.VMEM((4, 2 * rows, cols), bf16),
+            pltpu.VMEM((2, rows, cols), bf16),
+            pltpu.VMEM((2 * heads, rows, HEAD_DIM), f32),
+            pltpu.VMEM((2 * heads, rows, HEAD_DIM), f32),
+            pltpu.VMEM((2, rows, cols), bf16),
+            pltpu.VMEM((rows, cols), bf16),
+            pltpu.VMEM((4, 2 * wrows, wide), bf16),
+            pltpu.VMEM((rows, wide), f32),
+            pltpu.SemaphoreType.DMA((80,)),
+            pltpu.SemaphoreType.DMA((80,)),
+            pltpu.SemaphoreType.DMA((4,)),
+        ],
+        compiler_params=pltpu.CompilerParams(
+            collective_id=0, has_side_effects=True, vmem_limit_bytes=62 * 1024 * 1024
+        ),
+    )(cycle_order, queries, keys, values, out_weight, gate_row)
+
+
 def solution(mesh):
     in_specs = (
         P(("group", "frame", "sub"), "head"),
@@ -82,4 +481,6 @@
         P("group"),
     )
     out_specs = P(("group", "frame", "sub"), "head")
+    in_line = all(mesh.shape[a] == n for a, n in (("group", 2), ("frame", 4), ("head", 2), ("sub", 2)))
+    shards = line_shards if in_line else ring_shards
     return jax.shard_map(shards, mesh=mesh, in_specs=in_specs, out_specs=out_specs, check_vma=False)

time: 510 us -> 183 us (0.36)
  waiting for transfers between devices: 413 us -> 0 us
  Pallas kernels: 0 us -> 176 us
  matrix products: 48.1 us -> 1.1 us
  local copies, waits for them, and re-layouts: 22 us -> 5.61 us
  between operations: 13.2 us -> 0.03 us
  other arithmetic: 8.46 us -> 0.1 us
    ppermute x2 -> x0, waiting for transfers between devices: 246 us -> none  [from_behind(): lax.ppermute(array, axis, [(i, (i + by) % count) for i in range(count)])]
    pallas_call x0 -> x1, Pallas kernels: none -> 176 us  [line_shards(): pl.pallas_call(line_kernel, out_shape=jax.ShapeDtypeStruct((rows, wide),...]
    all_gather x3 -> x0, waiting for transfers between devices: 165 us -> none  [the longest x1 123 us: shards(): all_rows = lax.all_gather(out_weight, ('frame', 'sub'), axis=0, tiled=True)]
    dot_general x23 -> x2, matrix products: 48.1 us -> 1.1 us  [the longest x1 0.82 us: gate_of_slot(): jnp.dot(level_onehot[None, :], time_table, preferred_element_type=jnp.flo...]
    unnamed x13 -> x5, local copies, waits for them, and re-layouts: 10.5 us -> 2.95 us
    reduce_sum x11 -> x1, other arithmetic: 6.34 us -> 0.09 us  [gate_of_slot(): jnp.sum(action_match.astype(jnp.float32), axis=0).astype(jnp.bfloat16)]
  transfers between devices with their start and end apart: 5 -> 0, of which waited for: 5 -> 0; matrix products, arithmetic and copies ran while one was open for 2% -> 0% of each run, Pallas kernels for 0% -> 0%
where the time goes in v1:
time: 183 us
  Pallas kernels  176 us (96%)
  local copies, waits for them, and re-layouts  5.61 us (3%)
    pallas_call x1, Pallas kernels, line_shards(): pl.pallas_call(line_kernel, out_shape=jax.ShapeDtypeStruct((rows, wide),...  176 us

profile of v1, /device:TPU:1, one launch (start us, length us, event | category | flops | bytes accessed | tf_op | source)
XLA Modules:
  0.0 183.3 jit_solution(7877593573079982468)
XLA Ops:
  0.0 0.0 copy-start
  0.0 0.0 copy-start.1
  0.0 1.4 dynamic_slice.6
  1.4 0.7 dynamic-slice_bitcast_fusion
  2.0 0.1 convert_reduce_fusion
  2.1 0.0 copy-done
  2.1 0.3 convolution_reduce_fusion
  2.4 0.0 copy-done.1
  2.4 0.8 convolution_reduce_fusion.1
  3.3 0.6 add.11.gate
  3.9 176.4 %shard_map.91 = bf16[384,2560]{1,0:T(8,128)(2,1)} custom-call(s32[4]{0:T(128)} %cycle.1, bf16[384,1280]{1,0:T(8,128)(2,1)} %q.1, bf16[384,1280]{1,0:T(8,128)(2,1)} %k.1, bf16[384,1280]{1,0:T(8,128)(2,1)} %v.1, bf16[320,2560]{1,0:T(8,128)(2,1)} %w.1, f32[1,2560]{1,0:T(1,128)} %add.11.gate), custom_call_target="tpu_custom_call" | custom-call | tf_op jit(solution)/shard_map/pallas_call | solution.py:446
  180.3 2.9 %copy.11 = bf16[384,2560]{1,0:T(8,128)(2,1)} copy(bf16[384,2560]{1,0:T(8,128)(2,1)} %shard_map.91) | data formatting | bytes 3932160
  (2 shorter events, 0.0 us)
Async XLA Ops:
  0.0 2.1 %copy-start = (bf16[256,2560]{1,0:T(8,128)(2,1)S(1)}, bf16[256,2560]{1,0:T(8,128)(2,1)}, u32[]{:S(2)}) copy-start(bf16[256,2560]{1,0:T(8,128)(2,1)} %param.14) | copy-start | bytes 3932164
  0.0 2.4 %copy-start.1 = (bf16[50,2560]{1,0:T(8,128)(2,1)S(1)}, bf16[50,2560]{1,0:T(8,128)(2,1)}, u32[]{:S(2)}) copy-start(bf16[50,2560]{1,0:T(8,128)(2,1)} %param.13) | copy-start | bytes 768004

commit v2 on v1

--- a/solution.py
+++ b/solution.py
@@ -12,6 +12,9 @@
 ACTIONS = 256
 FWIN = 3
 PIECES = 5
+AHEAD = 2
+ROW_PARTS = 10
+W_AHEAD = 2 * AHEAD
 LOG2E = 1.4426950408889634
 MESH = pl.DeviceIdType.MESH
 
@@ -92,17 +95,17 @@
 
 
 def line_kernel(
-    cycle, q, k, v, w, gate, out,
-    kb, vb, qb, stat, acc, attf, aout, wf, pacc, send_sems, recv_sems, local_sems,
+    cycle, levels, actions, q, k, v, w, time_table, action_table, out,
+    kb, vb, qb, stat, acc, attf, aout, wf, pacc, gate, send_sems, recv_sems, local_sems,
 ):
     rows, cols = q.shape
     wrows, wide = w.shape
     half = wrows // 2
-    part = half // PIECES
+    part = half // ROW_PARTS
     heads = cols // HEAD_DIM
     per = heads // PIECES
     att_cols = per * HEAD_DIM
-    keys_n = 2 * rows
+    tile = 512
     scale = HEAD_DIM ** (-0.5) * LOG2E
 
     g, f, h, c = (lax.axis_index(name) for name in ("group", "frame", "head", "sub"))
@@ -151,6 +154,10 @@
     def kv_half(buf, block, cc):
         return buf.at[block, own_rows(0, rows, cc), :]
 
+    def kv_part(buf, block, cc, i):
+        lanes = pl.ds(pl.multiple_of(i * att_cols, HEAD_DIM), att_cols)
+        return buf.at[block, own_rows(0, rows, cc), lanes]
+
     def w_shard(block, cc):
         return wf.at[block, own_rows(0, wrows, cc), :]
 
@@ -163,10 +170,10 @@
     def att_part(ref, i):
         return ref.at[:, pl.ds(pl.multiple_of(i * att_cols, HEAD_DIM), att_cols)]
 
-    kv_z = lambda n, which: recvs("kvz" + n + which)
-    kv_s = lambda n, which: recvs("kvs" + n + which)
-    wz = {b: recvs("wz" + b, PIECES) for b in ("mate", "pi", "po")}
-    wy = {b: recvs("wy" + b, PIECES) for b in ("mate", "pi", "po")}
+    kv_z = lambda n, which: recvs("kvz" + n + which, 1 if which == "pi" else PIECES)
+    kv_s = lambda n, which: recvs("kvs" + n + which, 1 if which in ("i", "pi") else PIECES)
+    wz = {b: recvs("wz" + b, ROW_PARTS if b == "po" else 1) for b in ("mate", "pi", "po")}
+    wy = {b: recvs("wy" + b, ROW_PARTS if b == "po" else 1) for b in ("mate", "pi", "po")}
     ws = {b: recvs("ws" + b, 2) for b in ("mate", "pi", "po")}
     ws_own, rq = recvs("wsown"), recvs("q")
     ra, rx = recvs("ra", PIECES), recvs("rx", PIECES)
@@ -179,15 +186,35 @@
 
     def w_piece_to_y(b):
         src = w_piece(wblock[b], c, g)
-        copy(src, src, sends("wyp" + b, PIECES), wy[b], y_dev).start()
-
-    def w_part_to_y(b, i):
-        src = w_part(wblock[b], c, g, i)
-        copy(src, src, sends("wyp" + b, PIECES) + i, wy[b] + i, y_dev).start()
-
-    def w_part_to_mate(b, i):
-        src = w_part(wblock[b], c, g, i)
-        copy(src, src, sends("wout" + b, PIECES) + i, wz[b] + i, mate_dev).start()
+        copy(src, src, sends("wy" + b), wy[b], y_dev).start()
+
+    def last_w_to_y(i):
+        src = w_part(peer_out, c, g, i)
+        copy(src, src, sends("wypo", ROW_PARTS) + i, wy["po"] + i, y_dev).start()
+
+    def last_w_to_mate(i):
+        src = w_part(peer_out, c, g, i)
+        copy(src, src, sends("wout", ROW_PARTS) + i, wz["po"] + i, mate_dev).start()
+
+    def mate_w_to_peer(i):
+        src = w_part(mate, c, g, i)
+        copy(src, src, sends("w_mate_peer", ROW_PARTS) + i, wz["po"] + i, peer_dev).start()
+
+    def gate_rows():
+        @pl.loop(0, wide // tile)
+        def _(n):
+            lanes = pl.ds(pl.multiple_of(n * tile, tile), tile)
+            level_rows = time_table[:, lanes].astype(jnp.float32)
+            level_at = lax.broadcasted_iota(jnp.int32, level_rows.shape, 0)
+            total = jnp.sum(
+                jnp.where(level_at == levels[f], level_rows, 0.0), axis=0, keepdims=True
+            )
+            action_rows = action_table[:, lanes].astype(jnp.float32)
+            action_at = lax.broadcasted_iota(jnp.int32, action_rows.shape, 0)
+            times = jnp.zeros(action_rows.shape, jnp.float32)
+            for a in range(actions.shape[1]):
+                times += (action_at == actions[f, a]).astype(jnp.float32)
+            gate[:, lanes] = total + jnp.sum(times * action_rows, axis=0, keepdims=True)
 
     def valid_of(slot, block):
         distance = (slot - block + 4) % 4
@@ -256,51 +283,74 @@
             lane = lax.broadcasted_iota(jnp.int32, (rows, HEAD_DIM), 1)
             stat[i] = jnp.where(lane < 64, -1e30, 0.0)
 
+        gate_rows()
+
         for one in locals_:
             one.wait()
         for n, buf in (("k", kb), ("v", vb)):
             arrived(kv_half(buf, f, 1 - c), kv_s(n, "i"))
         units(0, f_in)
-        for n, buf in (("k", kb), ("v", vb)):
-            src = kv_half(buf, f_out, c)
-            arrived(src, kv_z(n, "o"))
-            copy(src, src, sends("o_peer" + n), kv_z(n, "po"), peer_dev).start()
-            copy(src, src, sends("o_sub" + n), kv_s(n, "o"), sub_dev).start()
+        own_w.wait()
+
+        def relay(i):
+            for n, buf in (("k", kb), ("v", vb)):
+                src = kv_part(buf, f_out, c, i)
+                arrived(src, kv_z(n, "o") + i)
+                send = sends("o_peer" + n, PIECES) + i
+                copy(src, src, send, kv_z(n, "po") + i, peer_dev).start()
+                copy(src, src, sends("o_sub" + n, PIECES) + i, kv_s(n, "o") + i, sub_dev).start()
+
+        src = w_piece(f, c, g)
+        copy(src, src, sends("w_own_peer"), wz["pi"], peer_dev).start()
+        for i in range(AHEAD):
+            relay(i)
         for n, buf in (("k", kb), ("v", vb)):
             src = kv_half(buf, peer_in, c)
             arrived(src, kv_z(n, "pi"))
             copy(src, src, sends("pi_sub" + n), kv_s(n, "pi"), sub_dev).start()
+        arrived(qb.at[1], rq)
         for n, buf in (("k", kb), ("v", vb)):
-            arrived(kv_half(buf, f_out, 1 - c), kv_s(n, "o"))
             arrived(kv_half(buf, peer_in, 1 - c), kv_s(n, "pi"))
-        units(0, jnp.where(side == 0, f_out, peer_in))
-        arrived(qb.at[1], rq)
-        units(1, f_out)
         units(1, peer_in)
-        arrived(w_piece(mate, c, g), wz["mate"])
-        w_piece_to_y("mate")
-        w_to_sub("mate", g, 0)
-        for n, buf in (("k", kb), ("v", vb)):
-            src = kv_half(buf, peer_out, c)
-            arrived(src, kv_z(n, "po"))
-            copy(src, src, sends("po_sub" + n), kv_s(n, "po"), sub_dev).start()
-        own_w.wait()
-
-        def w_to_peer(i):
-            src = w_part(f, c, g, i)
-            copy(src, src, sends("w_own_peer", PIECES) + i, wz["pi"] + i, peer_dev).start()
-
-        def mate_w_to_peer(i):
-            src = w_part(mate, c, g, i)
-            copy(src, src, sends("w_mate_peer", PIECES) + i, wz["po"] + i, peer_dev).start()
-
-        each_part(w_to_peer)
-        each_part(mate_w_to_peer)
-        for n, buf in (("k", kb), ("v", vb)):
-            arrived(kv_half(buf, peer_out, 1 - c), kv_s(n, "po"))
+        arrived(w_piece(peer_in, c, g), wz["pi"])
+        src = w_piece(peer_in, c, g)
+        copy(src, src, sends("w_pi_out"), wz["pi"], mate_dev).start()
+        w_piece_to_y("pi")
+        w_to_sub("pi", g, 0)
+        next_block = jnp.where(side == 0, f_out, peer_in)
         last_block = jnp.where(side == 0, peer_out, f_in)
 
         def last(i):
+            @pl.when(i + AHEAD < PIECES)
+            def _():
+                relay(i + AHEAD)
+
+            @pl.when(i + AHEAD == PIECES)
+            def _():
+                arrived(w_piece(mate, c, g), wz["mate"])
+                w_piece_to_y("mate")
+                w_to_sub("mate", g, 0)
+
+            @pl.when(i + AHEAD >= PIECES)
+            def _():
+                for j in range(2):
+                    mate_w_to_peer(2 * (i + AHEAD - PIECES) + j)
+
+            for n, buf in (("k", kb), ("v", vb)):
+                src = kv_part(buf, peer_out, c, i)
+                arrived(src, kv_z(n, "po") + i)
+                copy(src, src, sends("po_sub" + n, PIECES) + i, kv_s(n, "po") + i, sub_dev).start()
+            for n, buf in (("k", kb), ("v", vb)):
+                arrived(kv_part(buf, f_out, 1 - c, i), kv_s(n, "o") + i)
+
+            @pl.loop(0, per)
+            def _(j):
+                unit(1, f_out, i * per + j)
+                unit(0, next_block, i * per + j)
+
+            for n, buf in (("k", kb), ("v", vb)):
+                arrived(kv_part(buf, peer_out, 1 - c, i), kv_s(n, "po") + i)
+
             @pl.loop(0, per)
             def _(j):
                 unit(1, last_block, i * per + j, aout)
@@ -310,65 +360,94 @@
             copy(src, att_part(attf.at[h], i), sends("aout", PIECES) + i, ra + i, mate_dev).start()
             src = att_part(attf.at[h], i)
             copy(src, src, sends("ax", PIECES) + i, rx + i, x_dev).start()
-            arrived(w_part(peer_in, c, g, i), wz["pi"] + i)
-            w_part_to_mate("pi", i)
-            w_part_to_y("pi", i)
 
         each_part(last)
         arrived(w_piece(mate, c, 1 - g), wy["mate"])
         w_to_sub("mate", 1 - g, 1)
-        w_to_sub("pi", g, 0)
-
-        def po(i):
-            arrived(w_part(peer_out, c, g, i), wz["po"] + i)
-            w_part_to_mate("po", i)
-            w_part_to_y("po", i)
-
-        each_part(po)
 
     @pl.when(jnp.logical_not(inner))
     def _():
-        first = [
-            copy(k, kv_half(kb, f, c), sends("out_k"), kv_z("k", "o"), mate_dev),
-            copy(v, kv_half(vb, f, c), sends("out_v"), kv_z("v", "o"), mate_dev),
-        ]
-        for one in first:
-            one.start()
+        def kv_out(i):
+            lanes = pl.ds(pl.multiple_of(i * att_cols, HEAD_DIM), att_cols)
+            return [
+                copy(
+                    ref.at[:, lanes], kv_part(buf, f, c, i), sends("out_" + n, PIECES) + i,
+                    kv_z(n, "o") + i, mate_dev,
+                )
+                for n, ref, buf in (("k", k, kb), ("v", v, vb))
+            ]
+
+        def kv_start(i):
+            for one in kv_out(i):
+                one.start()
+
+        def kv_sent(i):
+            for one in kv_out(i):
+                one.wait_send()
+
+        q_copy = copy(q, qb.at[1], sends("out_q"), rq, mate_dev)
+        q_copy.start()
+        kv_start(0)
         w_to_partner.start()
         own_w.wait()
         arrived(w_piece(mate, c, g), wz["mate"])
         w_piece_to_y("mate")
         w_to_sub("mate", g, 0)
-        for one in first:
-            one.wait_send()
-        q_copy = copy(q, qb.at[1], sends("out_q"), rq, mate_dev)
-        q_copy.start()
         q_copy.wait_send()
+
+        @pl.loop(1, PIECES)
+        def _(i):
+            kv_start(i)
+            kv_sent(i - 1)
+
         src = w_piece(f, c, g)
         w_copy = copy(src, src, sends("out_w"), wz["mate"], mate_dev)
         w_copy.start()
+        kv_sent(PIECES - 1)
+        gate_rows()
         arrived(w_piece(mate, c, 1 - g), wy["mate"])
         w_to_sub("mate", 1 - g, 1)
+        arrived(w_piece(peer_in, c, g), wz["pi"])
+        w_piece_to_y("pi")
+        w_to_sub("pi", g, 0)
         w_copy.wait_send()
 
-        def pi(i):
+        def back(i):
             src = att_part(attf.at[h], i)
             arrived(src, ra + i)
             copy(src, src, sends("ax", PIECES) + i, rx + i, x_dev).start()
-            arrived(w_part(peer_in, c, g, i), wz["pi"] + i)
-            w_part_to_y("pi", i)
-
-        each_part(pi)
-        w_to_sub("pi", g, 0)
-
-        def po(i):
-            arrived(w_part(peer_out, c, g, i), wz["po"] + i)
-            w_part_to_y("po", i)
-
-        each_part(po)
-
-    w_to_sub("po", g, 0)
-    each_part(lambda i: arrived(w_part(peer_in, c, 1 - g, i), wy["pi"] + i))
+
+        each_part(back)
+
+    def last_w(i):
+        @pl.when(inner & (i + W_AHEAD < ROW_PARTS))
+        def _():
+            mate_w_to_peer(i + W_AHEAD)
+
+        arrived(w_part(peer_out, c, g, i), wz["po"] + i)
+
+        @pl.when(inner)
+        def _():
+            last_w_to_mate(i)
+
+        last_w_to_y(i)
+
+    depth = 2 * wrows
+
+    def product(block, lanes):
+        att_lanes = pl.ds(pl.multiple_of((block % 2) * depth, HEAD_DIM), depth)
+        return jnp.dot(
+            attf[block // 2, :, att_lanes], wf[block, :, lanes], preferred_element_type=jnp.float32
+        )
+
+    tiles = wide // tile
+    early = ROW_PARTS - tiles
+
+    @pl.loop(0, early)
+    def _(i):
+        last_w(i)
+
+    arrived(w_piece(peer_in, c, 1 - g), wy["pi"])
     w_to_sub("pi", 1 - g, 1)
     each_part(lambda i: arrived(att_part(attf.at[1 - h], i), rx + i))
     arrived(w_shard(f, 1 - c), ws_own)
@@ -376,26 +455,23 @@
         arrived(w_piece(wblock[b], 1 - c, g), ws[b])
         arrived(w_piece(wblock[b], 1 - c, 1 - g), ws[b] + 1)
 
-    depth = 2 * wrows
-    tile = 512
-
-    def product(block, lanes):
-        att_lanes = pl.ds(pl.multiple_of((block % 2) * depth, HEAD_DIM), depth)
-        return jnp.dot(
-            attf[block // 2, :, att_lanes], wf[block, :, lanes], preferred_element_type=jnp.float32
-        )
-
-    @pl.loop(0, wide // tile)
+    @pl.loop(0, tiles)
     def _(n):
+        last_w(n + early)
         lanes = pl.ds(pl.multiple_of(n * tile, tile), tile)
         pacc[:, lanes] = product(f, lanes) + product(mate, lanes) + product(peer_in, lanes)
 
-    each_part(lambda i: arrived(w_part(peer_out, c, 1 - g, i), wy["po"] + i))
+    w_to_sub("po", g, 0)
+
+    @pl.loop(0, ROW_PARTS)
+    def _(i):
+        arrived(w_part(peer_out, c, 1 - g, i), wy["po"] + i)
+
     w_to_sub("po", 1 - g, 1)
     arrived(w_piece(peer_out, 1 - c, g), ws["po"])
     arrived(w_piece(peer_out, 1 - c, 1 - g), ws["po"] + 1)
 
-    @pl.loop(0, wide // tile)
+    @pl.loop(0, tiles)
     def _(n):
         lanes = pl.ds(pl.multiple_of(n * tile, tile), tile)
         total = pacc[:, lanes] + product(peer_out, lanes)
@@ -408,28 +484,37 @@
     for b in ("mate", "pi", "po"):
         for which in range(2):
             sent(w_piece(0, 0, 0), "wsub" + b + str(which))
-    sent(w_piece(0, 0, 0), "wypmate")
+    sent(w_piece(0, 0, 0), "wymate")
+    sent(w_piece(0, 0, 0), "wypi")
 
     def common_sent(i):
         sent(att_part(aout, 0), "ax", i)
-        for b in ("pi", "po"):
-            sent(w_part(0, 0, 0, 0), "wyp" + b, i)
 
     each_part(common_sent)
+
+    @pl.loop(0, ROW_PARTS)
+    def _(i):
+        sent(w_part(0, 0, 0, 0), "wypo", i)
 
     @pl.when(inner)
     def _():
         for n in "kv":
-            for name in ("i_sub", "i_peer", "o_peer", "o_sub", "pi_sub", "po_sub"):
+            for name in ("i_sub", "i_peer", "pi_sub"):
                 sent(k, name + n)
-        sent(w_piece(0, 0, 0), "w_in_out")
+        for name in ("w_in_out", "w_own_peer", "w_pi_out"):
+            sent(w_piece(0, 0, 0), name)
 
         def inner_sent(i):
             sent(att_part(aout, 0), "aout", i)
-            for name in ("w_own_peer", "w_mate_peer", "woutpi", "woutpo"):
+            for name in ("o_peerk", "o_subk", "po_subk", "o_peerv", "o_subv", "po_subv"):
+                sent(att_part(aout, 0), name, i)
+
+        each_part(inner_sent)
+
+        @pl.loop(0, ROW_PARTS)
+        def _(i):
+            for name in ("w_mate_peer", "wout"):
                 sent(w_part(0, 0, 0, 0), name, i)
-
-        each_part(inner_sent)
 
     assert sends.used <= send_sems.shape[0] and recvs.used <= recv_sems.shape[0]
 
@@ -437,16 +522,17 @@
 def line_shards(
     queries, keys, values, out_weight, time_table, action_table, levels, actions, cycle_order
 ):
-    gate_row = gate_of_slot(time_table, action_table, levels, actions)
     rows, cols = queries.shape
     wrows, wide = out_weight.shape
     heads = cols // HEAD_DIM
     bf16, f32 = jnp.bfloat16, jnp.float32
-    vmem = pl.BlockSpec(memory_space=pltpu.VMEM)
+    vmem, smem, anywhere = (
+        pl.BlockSpec(memory_space=space) for space in (pltpu.VMEM, pltpu.SMEM, pl.ANY)
+    )
     return pl.pallas_call(
         line_kernel,
         out_shape=jax.ShapeDtypeStruct((rows, wide), bf16),
-        in_specs=[pl.BlockSpec(memory_space=pltpu.SMEM)] + [vmem] * 5,
+        in_specs=[smem] * 3 + [anywhere] * 4 + [vmem] * 2,
         out_specs=vmem,
         scratch_shapes=[
             pltpu.VMEM((4, 2 * rows, cols), bf16),
@@ -458,14 +544,17 @@
             pltpu.VMEM((rows, cols), bf16),
             pltpu.VMEM((4, 2 * wrows, wide), bf16),
             pltpu.VMEM((rows, wide), f32),
-            pltpu.SemaphoreType.DMA((80,)),
-            pltpu.SemaphoreType.DMA((80,)),
+            pltpu.VMEM((1, wide), f32),
+            pltpu.SemaphoreType.DMA((120,)),
+            pltpu.SemaphoreType.DMA((120,)),
             pltpu.SemaphoreType.DMA((4,)),
         ],
         compiler_params=pltpu.CompilerParams(
             collective_id=0, has_side_effects=True, vmem_limit_bytes=62 * 1024 * 1024
         ),
-    )(cycle_order, queries, keys, values, out_weight, gate_row)
+    )(
+        cycle_order, levels, actions, queries, keys, values, out_weight, time_table, action_table
+    )
 
 
 def solution(mesh):

time: 183 us -> 159 us (0.87)
  Pallas kernels: 176 us -> 155 us
  local copies, waits for them, and re-layouts: 5.61 us -> 2.94 us
    pallas_call x1, Pallas kernels: 176 us -> 155 us  [line_shards(): pl.pallas_call(line_kernel, out_shape=jax.ShapeDtypeStruct((rows, wide),...]
where the time goes in v2:
time: 159 us; the launch traced here: 158 us
  Pallas kernels  155 us (97%)
  local copies, waits for them, and re-layouts  2.94 us (2%)
    pallas_call x1, Pallas kernels, line_shards(): pl.pallas_call(line_kernel, out_shape=jax.ShapeDtypeStruct((rows, wide),...  155 us

profile of v2, /device:TPU:1, one launch (start us, length us, event | category | flops | bytes accessed | tf_op | source)
XLA Modules:
  0.0 158.4 jit_solution(2852021065101819688)
XLA Ops:
  0.0 155.4 %shard_map.91 = bf16[384,2560]{1,0:T(8,128)(2,1)} custom-call(s32[4]{0:T(128)} %cycle.1, s32[4]{0:T(128)} %levels.1, s32[4,4]{1,0:T(4,128)} %actions.1, bf16[384,1280]{1,0:T(8,128)(2,1)} %q.1, bf16[384,1280]{1,0:T(8,128)(2,1)} %k.1, bf16[384,1280]{1,0:T(8,128)(2,1)} %v.1, bf16[320,2560]{1,0:T(8,128)(2,1)} %w.1, bf16[50,2560]{1,0:T(8,128)(2,1)} %time_table.1, ...), custom_call_target="tpu_custom_call" | custom-call | tf_op jit(solution)/shard_map/pallas_call | solution.py:532
  155.4 2.9 %copy.11 = bf16[384,2560]{1,0:T(8,128)(2,1)} copy(bf16[384,2560]{1,0:T(8,128)(2,1)} %shard_map.91) | data formatting | bytes 3932160

commit v3 on v2

--- a/solution.py
+++ b/solution.py
@@ -15,6 +15,7 @@
 AHEAD = 2
 ROW_PARTS = 10
 W_AHEAD = 2 * AHEAD
+GANG = 2
 LOG2E = 1.4426950408889634
 MESH = pl.DeviceIdType.MESH
 
@@ -106,6 +107,7 @@
     per = heads // PIECES
     att_cols = per * HEAD_DIM
     tile = 512
+    keys_n = 2 * rows
     scale = HEAD_DIM ** (-0.5) * LOG2E
 
     g, f, h, c = (lax.axis_index(name) for name in ("group", "frame", "head", "sub"))
@@ -220,36 +222,45 @@
         distance = (slot - block + 4) % 4
         return cycle[block] == cycle[slot] - distance
 
-    def unit(si, block, head, finish=None):
-        slot = jnp.where(si == 0, f_in, f_out)
-        valid = valid_of(slot, block)
-        lanes = pl.ds(pl.multiple_of(head * HEAD_DIM, HEAD_DIM), HEAD_DIM)
-        si_head = si * heads + head
-        scores = lax.dot_general(
-            qb[si, :, lanes], kb[block, :, lanes], (((1,), (1,)), ((), ())),
-            preferred_element_type=jnp.float32,
-        )
-        old = stat[si_head]
-        old_max, old_total = old[:, :1], old[:, 64:65]
-        block_max = jnp.where(valid, jnp.max(scores, axis=1, keepdims=True), -1e30)
-        new_max = jnp.maximum(old_max, block_max)
-        weights = jnp.exp2((scores - jnp.where(valid, new_max, 1e30)) * scale)
-        fade = jnp.exp2((old_max - new_max) * scale)
-        total = old_total * fade + jnp.sum(weights, axis=1, keepdims=True)
-        mixed = acc[si_head] * fade + jnp.dot(
-            weights.astype(jnp.bfloat16), vb[block, :, lanes], preferred_element_type=jnp.float32
-        )
-        if finish is None:
-            acc[si_head] = mixed
-            lane = lax.broadcasted_iota(jnp.int32, (rows, HEAD_DIM), 1)
-            stat[si_head] = jnp.where(lane < 64, new_max, total)
-        else:
-            finish[:, lanes] = (mixed / total).astype(jnp.bfloat16)
+    def attend(items):
+        lanes = [
+            pl.ds(pl.multiple_of(head * HEAD_DIM, HEAD_DIM), HEAD_DIM) for _, _, head, _ in items
+        ]
+        scores = [
+            lax.dot_general(
+                qb[si, :, at], kb[block, :, at], (((1,), (1,)), ((), ())),
+                preferred_element_type=jnp.float32,
+            )
+            for (si, block, _, _), at in zip(items, lanes)
+        ]
+        ones = jnp.ones((keys_n, HEAD_DIM), jnp.bfloat16)
+        results = []
+        for (si, block, head, _), at, score in zip(items, lanes, scores):
+            valid = valid_of(jnp.where(si == 0, f_in, f_out), block)
+            old_max = stat[si * heads + head]
+            block_max = jnp.where(valid, jnp.max(score, axis=1, keepdims=True), -1e30)
+            new_max = jnp.maximum(old_max, block_max)
+            base = jnp.where(valid, new_max, 1e30)
+            weights = jnp.exp2((score - jnp.concatenate([base] * (keys_n // HEAD_DIM), 1)) * scale)
+            fade = jnp.exp2((old_max - new_max) * scale)
+            values = jnp.concatenate([vb[block, :, at], ones], 1)
+            mixed = jnp.dot(
+                weights.astype(jnp.bfloat16), values, preferred_element_type=jnp.float32
+            )
+            mixed += acc[si * heads + head] * jnp.concatenate([fade, fade], 1)
+            results.append((new_max, mixed))
+        for (si, _, head, finish), at, (new_max, mixed) in zip(items, lanes, results):
+            if finish is None:
+                acc[si * heads + head] = mixed
+                stat[si * heads + head] = new_max
+            else:
+                rounded = (mixed[:, :HEAD_DIM] / mixed[:, HEAD_DIM:]).astype(jnp.bfloat16)
+                finish[:, at] = rounded
 
     def units(si, block):
-        @pl.loop(0, heads)
-        def _(head):
-            unit(si, block, head)
+        @pl.loop(0, heads // GANG)
+        def _(n):
+            attend([(si, block, n * GANG + j, None) for j in range(GANG)])
 
     def each_part(body):
         @pl.loop(0, PIECES)
@@ -279,9 +290,8 @@
 
         @pl.loop(0, 2 * heads)
         def _(i):
-            acc[i] = jnp.zeros((rows, HEAD_DIM), jnp.float32)
-            lane = lax.broadcasted_iota(jnp.int32, (rows, HEAD_DIM), 1)
-            stat[i] = jnp.where(lane < 64, -1e30, 0.0)
+            acc[i] = jnp.zeros((rows, 2 * HEAD_DIM), jnp.float32)
+            stat[i] = jnp.full((rows, HEAD_DIM), -1e30, jnp.float32)
 
         gate_rows()
 
@@ -345,16 +355,16 @@
 
             @pl.loop(0, per)
             def _(j):
-                unit(1, f_out, i * per + j)
-                unit(0, next_block, i * per + j)
+                head = i * per + j
+                attend([(1, f_out, head, None), (0, next_block, head, None)])
 
             for n, buf in (("k", kb), ("v", vb)):
                 arrived(kv_part(buf, peer_out, 1 - c, i), kv_s(n, "po") + i)
 
             @pl.loop(0, per)
             def _(j):
-                unit(1, last_block, i * per + j, aout)
-                unit(0, peer_out, i * per + j, attf.at[h])
+                head = i * per + j
+                attend([(1, last_block, head, aout), (0, peer_out, head, attf.at[h])])
 
             src = att_part(aout, i)
             copy(src, att_part(attf.at[h], i), sends("aout", PIECES) + i, ra + i, mate_dev).start()
@@ -539,7 +549,7 @@
             pltpu.VMEM((4, 2 * rows, cols), bf16),
             pltpu.VMEM((2, rows, cols), bf16),
             pltpu.VMEM((2 * heads, rows, HEAD_DIM), f32),
-            pltpu.VMEM((2 * heads, rows, HEAD_DIM), f32),
+            pltpu.VMEM((2 * heads, rows, 2 * HEAD_DIM), f32),
             pltpu.VMEM((2, rows, cols), bf16),
             pltpu.VMEM((rows, cols), bf16),
             pltpu.VMEM((4, 2 * wrows, wide), bf16),

time: 159 us -> 155 us (0.975)
  Pallas kernels: 155 us -> 151 us
    pallas_call x1, Pallas kernels: 155 us -> 151 us  [line_shards(): pl.pallas_call(line_kernel, out_shape=jax.ShapeDtypeStruct((rows, wide),...]
where the time goes in v3:
time: 155 us; the launch traced here: 154 us
  Pallas kernels  151 us (97%)
  local copies, waits for them, and re-layouts  2.94 us (2%)
    pallas_call x1, Pallas kernels, line_shards(): pl.pallas_call(line_kernel, out_shape=jax.ShapeDtypeStruct((rows, wide),...  151 us

profile of v3, /device:TPU:1, one launch (start us, length us, event | category | flops | bytes accessed | tf_op | source)
XLA Modules:
  0.0 154.4 jit_solution(2800869737475112519)
XLA Ops:
  0.0 151.4 %shard_map.91 = bf16[384,2560]{1,0:T(8,128)(2,1)} custom-call(s32[4]{0:T(128)} %cycle.1, s32[4]{0:T(128)} %levels.1, s32[4,4]{1,0:T(4,128)} %actions.1, bf16[384,1280]{1,0:T(8,128)(2,1)} %q.1, bf16[384,1280]{1,0:T(8,128)(2,1)} %k.1, bf16[384,1280]{1,0:T(8,128)(2,1)} %v.1, bf16[320,2560]{1,0:T(8,128)(2,1)} %w.1, bf16[50,2560]{1,0:T(8,128)(2,1)} %time_table.1, ...), custom_call_target="tpu_custom_call" | custom-call | tf_op jit(solution)/shard_map/pallas_call | solution.py:542
  151.4 2.9 %copy.11 = bf16[384,2560]{1,0:T(8,128)(2,1)} copy(bf16[384,2560]{1,0:T(8,128)(2,1)} %shard_map.91) | data formatting | bytes 3932160

commit v4 on v3

--- a/solution.py
+++ b/solution.py
@@ -96,8 +96,8 @@
 
 
 def line_kernel(
-    cycle, levels, actions, q, k, v, w, time_table, action_table, out,
-    kb, vb, qb, stat, acc, attf, aout, wf, pacc, gate, send_sems, recv_sems, local_sems,
+    cycle, levels, actions, q, k, v, w, time_table, action_rows_in, out,
+    kb, vb, qb, stat, acc, attf, aout, wf, pacc, gate, action_table, send_sems, recv_sems, local_sems,
 ):
     rows, cols = q.shape
     wrows, wide = w.shape
@@ -176,7 +176,7 @@
     kv_s = lambda n, which: recvs("kvs" + n + which, 1 if which in ("i", "pi") else PIECES)
     wz = {b: recvs("wz" + b, ROW_PARTS if b == "po" else 1) for b in ("mate", "pi", "po")}
     wy = {b: recvs("wy" + b, ROW_PARTS if b == "po" else 1) for b in ("mate", "pi", "po")}
-    ws = {b: recvs("ws" + b, 2) for b in ("mate", "pi", "po")}
+    ws = {b: recvs("ws" + b, 4 if b == "po" else 2) for b in ("mate", "pi", "po")}
     ws_own, rq = recvs("wsown"), recvs("q")
     ra, rx = recvs("ra", PIECES), recvs("rx", PIECES)
     wblock = {"mate": mate, "pi": peer_in, "po": peer_out}
@@ -186,6 +186,14 @@
         one = copy(src, src, sends("wsub" + b + str(which)), ws[b] + which, sub_dev)
         one.start()
 
+    def last_w_to_sub(gg, which, i):
+        src = wf.at[peer_out, own_rows(c * wrows + gg * half, half // 2, i), :]
+        copy(src, src, sends("wlast" + str(which), 2) + i, ws["po"] + 2 * which + i, sub_dev).start()
+
+    def last_w_from_sub(gg, which, i):
+        dst = wf.at[peer_out, own_rows((1 - c) * wrows + gg * half, half // 2, i), :]
+        arrived(dst, ws["po"] + 2 * which + i)
+
     def w_piece_to_y(b):
         src = w_piece(wblock[b], c, g)
         copy(src, src, sends("wy" + b), wy[b], y_dev).start()
@@ -202,7 +210,11 @@
         src = w_part(mate, c, g, i)
         copy(src, src, sends("w_mate_peer", ROW_PARTS) + i, wz["po"] + i, peer_dev).start()
 
+    own_actions = pltpu.make_async_copy(action_rows_in, action_table, local_sems.at[4])
+
     def gate_rows():
+        own_actions.wait()
+
         @pl.loop(0, wide // tile)
         def _(n):
             lanes = pl.ds(pl.multiple_of(n * tile, tile), tile)
@@ -269,6 +281,7 @@
 
     own_w = pltpu.make_async_copy(w, w_shard(f, c), local_sems.at[0])
     own_w.start()
+    own_actions.start()
     w_to_partner = copy(w, w_shard(f, c), sends("wown"), ws_own, sub_dev)
 
     @pl.when(inner)
@@ -335,7 +348,7 @@
             def _():
                 relay(i + AHEAD)
 
-            @pl.when(i + AHEAD == PIECES)
+            @pl.when(i == 1)
             def _():
                 arrived(w_piece(mate, c, g), wz["mate"])
                 w_piece_to_y("mate")
@@ -405,14 +418,18 @@
         w_to_sub("mate", g, 0)
         q_copy.wait_send()
 
+        src = w_piece(f, c, g)
+        w_copy = copy(src, src, sends("out_w"), wz["mate"], mate_dev)
+
         @pl.loop(1, PIECES)
         def _(i):
+            @pl.when(i == 3)
+            def _():
+                w_copy.start()
+
             kv_start(i)
             kv_sent(i - 1)
 
-        src = w_piece(f, c, g)
-        w_copy = copy(src, src, sends("out_w"), wz["mate"], mate_dev)
-        w_copy.start()
         kv_sent(PIECES - 1)
         gate_rows()
         arrived(w_piece(mate, c, 1 - g), wy["mate"])
@@ -457,6 +474,7 @@
     def _(i):
         last_w(i)
 
+    last_w_to_sub(g, 0, 0)
     arrived(w_piece(peer_in, c, 1 - g), wy["pi"])
     w_to_sub("pi", 1 - g, 1)
     each_part(lambda i: arrived(att_part(attf.at[1 - h], i), rx + i))
@@ -471,15 +489,17 @@
         lanes = pl.ds(pl.multiple_of(n * tile, tile), tile)
         pacc[:, lanes] = product(f, lanes) + product(mate, lanes) + product(peer_in, lanes)
 
-    w_to_sub("po", g, 0)
-
-    @pl.loop(0, ROW_PARTS)
-    def _(i):
-        arrived(w_part(peer_out, c, 1 - g, i), wy["po"] + i)
-
-    w_to_sub("po", 1 - g, 1)
-    arrived(w_piece(peer_out, 1 - c, g), ws["po"])
-    arrived(w_piece(peer_out, 1 - c, 1 - g), ws["po"] + 1)
+    last_w_to_sub(g, 0, 1)
+    for i in range(2):
+
+        @pl.loop(i * (ROW_PARTS // 2), (i + 1) * (ROW_PARTS // 2))
+        def _(j):
+            arrived(w_part(peer_out, c, 1 - g, j), wy["po"] + j)
+
+        last_w_to_sub(1 - g, 1, i)
+    for which, gg in ((0, g), (1, 1 - g)):
+        for i in range(2):
+            last_w_from_sub(gg, which, i)
 
     @pl.loop(0, tiles)
     def _(n):
@@ -491,9 +511,12 @@
         copy(src, src, sends(name) + offset, 0, sub_dev).wait_send()
 
     sent(w, "wown")
-    for b in ("mate", "pi", "po"):
+    for b in ("mate", "pi"):
         for which in range(2):
             sent(w_piece(0, 0, 0), "wsub" + b + str(which))
+    for which in range(2):
+        for i in range(2):
+            sent(wf.at[0, own_rows(0, half // 2, 0), :], "wlast" + str(which), i)
     sent(w_piece(0, 0, 0), "wymate")
     sent(w_piece(0, 0, 0), "wypi")
 
@@ -542,7 +565,7 @@
     return pl.pallas_call(
         line_kernel,
         out_shape=jax.ShapeDtypeStruct((rows, wide), bf16),
-        in_specs=[smem] * 3 + [anywhere] * 4 + [vmem] * 2,
+        in_specs=[smem] * 3 + [anywhere] * 4 + [vmem, anywhere],
         out_specs=vmem,
         scratch_shapes=[
             pltpu.VMEM((4, 2 * rows, cols), bf16),
@@ -555,9 +578,10 @@
             pltpu.VMEM((4, 2 * wrows, wide), bf16),
             pltpu.VMEM((rows, wide), f32),
             pltpu.VMEM((1, wide), f32),
+            pltpu.VMEM(action_table.shape, bf16),
             pltpu.SemaphoreType.DMA((120,)),
             pltpu.SemaphoreType.DMA((120,)),
-            pltpu.SemaphoreType.DMA((4,)),
+            pltpu.SemaphoreType.DMA((5,)),
         ],
         compiler_params=pltpu.CompilerParams(
             collective_id=0, has_side_effects=True, vmem_limit_bytes=62 * 1024 * 1024

time: 155 us -> 154 us (level)
  no operation moved by 1% of the time
where the time goes in v4:
time: 154 us; the launch traced here: 153 us
  Pallas kernels  150 us (97%)
  local copies, waits for them, and re-layouts  2.94 us (2%)
    pallas_call x1, Pallas kernels, line_shards(): pl.pallas_call(line_kernel, out_shape=jax.ShapeDtypeStruct((rows, wide),...  150 us

profile of v4, /device:TPU:1, one launch (start us, length us, event | category | flops | bytes accessed | tf_op | source)
XLA Modules:
  0.0 153.5 jit_solution(2246717835050885763)
XLA Ops:
  0.0 150.5 %shard_map.91 = bf16[384,2560]{1,0:T(8,128)(2,1)} custom-call(s32[4]{0:T(128)} %cycle.1, s32[4]{0:T(128)} %levels.1, s32[4,4]{1,0:T(4,128)} %actions.1, bf16[384,1280]{1,0:T(8,128)(2,1)} %q.1, bf16[384,1280]{1,0:T(8,128)(2,1)} %k.1, bf16[384,1280]{1,0:T(8,128)(2,1)} %v.1, bf16[320,2560]{1,0:T(8,128)(2,1)} %w.1, bf16[50,2560]{1,0:T(8,128)(2,1)} %time_table.1, ...), custom_call_target="tpu_custom_call" | custom-call | tf_op jit(solution)/shard_map/pallas_call | solution.py:565
  150.5 2.9 %copy.11 = bf16[384,2560]{1,0:T(8,128)(2,1)} copy(bf16[384,2560]{1,0:T(8,128)(2,1)} %shard_map.91) | data formatting | bytes 3932160
